TPU v7x, 32 devices: a whole 2x2x4 slice. The times are simulated.
32 devices in a mesh: grp: 4 (over z), feat: 8 (over y, x, core).
Axes of the slice: x: 2, y: 2, z: 4, core: 2. Of those that a mesh axis runs over, the one named last changes fastest.
Arguments:
- features: bfloat16 [8192, 512], P(('grp', 'feat')), may hold values from -6 to 6
- adj_tiles: bfloat16 [64, 16, 128, 128], P(('grp', 'feat')), may hold values from 0.0099487305 to 1
- src_block: int32 [64, 16], P(('grp', 'feat')), may hold values from 0 to 15, as said below
- counts: int32 [64], P(('grp', 'feat')), may hold values from 1 to 16, as said below
- w_self: bfloat16 [512, 512], replicated, may hold values from -0.25 to 0.25
- w_neigh: bfloat16 [512, 512], replicated, may hold values from -0.25 to 0.25
- multiplier: float32 [512], replicated, may hold values from 0.5 to 2
- bit_shift: int32 [512], replicated, may hold values from 0 to 2
- cotangent: bfloat16 [8192, 512], P(('grp', 'feat')), may hold values from -6 to 6
Outputs:
- output: bfloat16 [8192, 512], P(('grp', 'feat'))
- grad_features: bfloat16 [8192, 512], P(('grp', 'feat'))
- grad_self: float32 [512, 512], replicated
- grad_neigh: float32 [512, 512], replicated
Inputs may be any that keep to these rules, and one draw needn't show every extreme that they name: src_block[i, k] is a block of block i's own group, held by a device at most 2 positions from block i's device in the group's cyclic order of devices (block i is held by device (i % 16) // 2 of its group, which holds 2 consecutive blocks); the distance 2 is reached in both directions in every draw. Slots k >= counts[i] take no part.
All inputs are finite; a program needn't handle non-finite values.
Results may differ from a plain program's by a relative error of at most 0.0059.
Values may be sent and summed in bfloat16 or wider, within the bound.
A program may use at most 64 MiB of HBM per device.

v0:
```python
import functools
import math

import jax
import jax.numpy as jnp
from jax import lax
from jax.experimental import pallas as pl
from jax.experimental.pallas import tpu as pltpu
from jax.sharding import PartitionSpec as P

SPAN = 2
WIN = 2 * SPAN + 1
MESH = pl.DeviceIdType.MESH
STRIP = 32
CHUNKS = 8
SPLIT = 3


def dot_nn(a, b):
    return jnp.dot(a, b, preferred_element_type=jnp.float32)


def dot_tn(a, b):
    return lax.dot_general(a, b, (((0,), (0,)), ((), ())), preferred_element_type=jnp.float32)


def dot_nt(a, b):
    return lax.dot_general(a, b, (((1,), (1,)), ((), ())), preferred_element_type=jnp.float32)


def strips(rows, body, step=STRIP):
    def run(i, carry):
        body(pl.ds(pl.multiple_of(i * step, step), step))
        return carry

    lax.fori_loop(0, rows // step, run, 0)


def kernel(
    n_feat, n_grp, fine,
    src_ref, cnt_ref, feat_hbm, adj_hbm, ws_hbm, wn_hbm, mult_hbm, shift_hbm, cot_hbm,
    out_hbm, gfeat_hbm, grads_hbm,
    out_ref, gfeat_ref,
    adj_ref, ws_ref, wn_ref, mult_ref, shift_ref, cot_ref,
    pool, dense, dsum, inv, summed, preact, both, gpre,
    buf1, in2, buf2, in3, full,
    back, term_out, term_sum, own_grad, term_in,
    load_s, store_s, halo_s, halo_r, term_s, term_r,
    pair_s, pair_r, rs2_s, rs2_r, rs3_s, rs3_r,
    ag1_s, ag1_r, ag2_s, ag2_r, ag3_s, ag3_r,
):
    n_chip = n_feat // 2
    square = n_chip == 4
    me = lax.axis_index("feat")
    grp = lax.axis_index("grp")
    core = lax.rem(me, 2)
    chip = me // 2
    odd = lax.rem(chip, 2)
    partner = me + 1 - 2 * core
    num_blocks, num_slots, block_len, _ = adj_ref.shape
    rows, width = feat_hbm.shape
    lanes = buf1.shape[1]
    ahead = lax.rem(me + 2, n_feat)
    behind = lax.rem(me + n_feat - 2, n_feat)
    chip_peers = [2 * lax.rem(chip + j, n_chip) + core for j in range(1, n_chip)]
    grp_peers = [lax.rem(grp + j, n_grp) for j in range(1, n_grp)]
    x_slot = 4 - 4 * odd
    y_slot = 4 * odd
    x_peer = 2 * (chip + 1 - 2 * odd) + core
    y_peer = 2 * lax.rem(chip + 2, n_chip) + core

    def to_feat(peer):
        return (grp, peer)

    def to_grp(peer):
        return (peer, me)

    sent = []

    def send(src, dst, ssem, rsem, device):
        copy = pltpu.make_async_remote_copy(
            src_ref=src, dst_ref=dst, send_sem=ssem, recv_sem=rsem, device_id=device, device_id_type=MESH
        )
        copy.start()
        sent.append(copy)

    def landed(dst, rsem):
        pltpu.make_async_remote_copy(
            src_ref=dst, dst_ref=dst, send_sem=rsem, recv_sem=rsem, device_id=to_feat(partner), device_id_type=MESH
        ).wait_recv()

    loads = [
        pltpu.make_async_copy(src, dst, load_s.at[i])
        for i, (src, dst) in enumerate(
            (
                (feat_hbm, both.at[0]), (adj_hbm, adj_ref), (ws_hbm, ws_ref), (wn_hbm, wn_ref),
                (mult_hbm, mult_ref), (shift_hbm, shift_ref), (cot_hbm, cot_ref),
            )
        )
    ]
    barrier = pltpu.get_barrier_semaphore()
    partners = [to_feat(partner)] + [to_feat(p) for p in chip_peers] + [to_grp(p) for p in grp_peers]
    for device in partners:
        pl.semaphore_signal(barrier, inc=1, device_id=device, device_id_type=MESH)
    for load in loads:
        load.start()
    loads[0].wait()
    pl.semaphore_wait(barrier, len(partners))

    near = 3 - 2 * core
    passed = 1 + 2 * core
    far = 4 - 4 * core
    other = 4 * core
    step = rows // CHUNKS
    chunks = [pl.ds(c * step, step) for c in range(CHUNKS)]
    if square:
        for c, at in enumerate(chunks):
            send(both.at[0, at], pool.at[y_slot, at], halo_s.at[0, c], halo_r.at[y_slot, c], to_feat(x_peer))
    else:
        for c, at in enumerate(chunks):
            send(both.at[0, at], pool.at[0, at], halo_s.at[0, c], halo_r.at[0, c], to_feat(ahead))
            send(both.at[0, at], pool.at[4, at], halo_s.at[1, c], halo_r.at[4, c], to_feat(behind))
    send(both.at[0], both.at[2], halo_s.at[2, 0], halo_r.at[SPAN, 0], to_feat(partner))

    dsum[...] = jnp.zeros_like(dsum)
    loads[1].wait()

    def build(piece, carry):
        owner = lax.rem(me + piece - SPAN + n_feat, n_feat)
        for b in range(num_blocks):
            dst_rows = slice(b * block_len, (b + 1) * block_len)
            for h in range(num_blocks):
                source = owner * num_blocks + h
                acc = jnp.zeros((block_len, block_len), jnp.float32)
                for k in range(num_slots):
                    hit = jnp.logical_and(src_ref[b, k] == source, cnt_ref[b] > k)
                    acc = acc + adj_ref[b, k].astype(jnp.float32) * jnp.where(hit, 1.0, 0.0)
                dsum[dst_rows, :] += acc
                dense[piece, dst_rows, h * block_len : (h + 1) * block_len] = acc.astype(jnp.bfloat16)
        return carry

    def relay():
        for c, at in enumerate(chunks):
            landed(pool.at[x_slot, at], halo_r.at[x_slot, c])
            if square:
                send(pool.at[x_slot, at], pool.at[y_slot, at], halo_s.at[1, c], halo_r.at[y_slot, c], to_feat(y_peer))

    lax.fori_loop(0, SPLIT, build, 0)
    relay()
    lax.fori_loop(SPLIT, WIN, build, 0)
    inv[...] = jnp.broadcast_to(lax.rsqrt(jnp.sum(dsum[...], axis=1, keepdims=True)), inv.shape)
    loads[2].wait()
    preact[...] = dot_nn(both[0], ws_ref[...])
    summed[...] = dot_nn(dense[SPAN], both[0])
    landed(both.at[2], halo_r.at[SPAN, 0])
    summed[...] += dot_nn(dense[near], both[2])
    summed[...] += dot_nn(dense[x_slot], pool[x_slot])
    for c, at in enumerate(chunks):
        landed(pool.at[y_slot, at], halo_r.at[y_slot, c])
        send(pool.at[far, at], pool.at[near, at], halo_s.at[3, c], halo_r.at[near, c], to_feat(partner))
    summed[...] += dot_nn(dense[y_slot], pool[y_slot])
    for load in loads[3:]:
        load.wait()
    for c, at in enumerate(chunks):
        landed(pool.at[passed, at], halo_r.at[passed, c])
    summed[...] += dot_nn(dense[passed], pool[passed])

    def aggregate(at):
        both[1, at, :] = (summed[at, :] * inv[at, :1]).astype(jnp.bfloat16)

    strips(rows, aggregate)
    send(both.at[1], both.at[3], pair_s.at[0], pair_r.at[0], to_feat(partner))
    preact[...] += dot_nn(both[1], wn_ref[...])
    mult_ref[...] = mult_ref[...] * jnp.exp2(-shift_ref[...].astype(jnp.float32))

    tstep = rows // 2
    halves = [pl.ds(c * tstep, tstep) for c in range(2)]

    def activate(at):
        scale = mult_ref[...]
        scaled = preact[at, :] * scale
        gate = 1.0 / (1.0 + jnp.exp(-scaled))
        out_ref[at, :] = (scaled * gate).astype(jnp.bfloat16)
        gpre[0, at, :] = (
            cot_ref[at, :].astype(jnp.float32) * gate * (1.0 + scaled * (1.0 - gate)) * scale
        ).astype(jnp.bfloat16)

    for c, at in enumerate(halves):
        strips(tstep, lambda part, c=c: activate(pl.ds(c * tstep + part.start, part.size)))
        send(gpre.at[0, at], gpre.at[1, at], pair_s.at[1 + c], pair_r.at[1 + c], to_feat(partner))
    stores = []

    def store(src, dst):
        copy = pltpu.make_async_copy(src, dst, store_s.at[len(stores)])
        copy.start()
        stores.append(copy)

    store(out_ref, out_hbm)

    pulled = dot_nt(gpre[0], wn_ref[...])
    back[...] = (pulled * inv[:, :1]).astype(jnp.bfloat16)
    term_out[passed] = dot_tn(dense[passed], back[...]).astype(jnp.bfloat16)
    send(term_out.at[passed], term_in.at[2], term_s.at[0, 0], term_r.at[2, 0], to_feat(partner))

    half = buf1.shape[0]
    c2 = buf2.shape[0]
    c3 = c2 // n_grp
    order = [lax.rem(chip + j, n_chip) for j in range(1, n_chip + 1)]
    if fine:
        owners = [lax.rem(grp + 1 + q, n_grp) for q in range(n_grp)]
        cuts = [(pl.multiple_of(o * c3, c3), c3) for o in owners]
    else:
        cuts = [(0, c2)]

    def share_out(j):
        for q, (first, size) in enumerate(cuts):
            src = buf1.at[pl.ds(pl.multiple_of(order[j] * c2 + first, 16), size)]
            send(src, in2.at[j, pl.ds(first, size)], rs2_s.at[j, q], rs2_r.at[j, q], to_feat(chip_peers[j]))

    landed(both.at[3], pair_r.at[0])
    for c, at in enumerate(halves):
        landed(gpre.at[1, at], pair_r.at[1 + c])
    if lanes == gpre.shape[2]:
        for j in range(n_chip):
            at = pl.ds(pl.multiple_of(order[j] * c2, c2), c2)
            part = dot_tn(both[core, :, at], gpre[0]) + dot_tn(both[2 + core, :, at], gpre[1])
            buf1[at, :] = part.astype(jnp.bfloat16)
            if j < n_chip - 1:
                share_out(j)
    else:
        part = dot_tn(both[core], gpre[0]) + dot_tn(both[2 + core], gpre[1])
        for j in range(gpre.shape[2] // lanes):
            buf1[j * width : (j + 1) * width, :] = part[:, j * lanes : (j + 1) * lanes].astype(jnp.bfloat16)
        for j in range(n_chip - 1):
            share_out(j)

    term_sum[0] = dot_tn(dense[x_slot], back[...])
    term_sum[1] = dot_tn(dense[y_slot], back[...])
    landed(term_in.at[2], term_r.at[2, 0])
    through = lax.rem(core + chip, 2)
    term_sum[through] += term_in[2].astype(jnp.float32)
    for c, at in enumerate(halves):
        term_out[y_slot, at, :] = term_sum[1, at, :].astype(jnp.bfloat16)
        if square:
            send(term_out.at[y_slot, at], term_in.at[1, at], term_s.at[1, c], term_r.at[1, c], to_feat(y_peer))
        else:
            target = lax.rem(me + y_slot - 2 + n_feat, n_feat)
            send(term_out.at[y_slot, at], term_in.at[odd, at], term_s.at[1, c], term_r.at[odd, c], to_feat(target))
    term_out[near] = dot_tn(dense[near], back[...]).astype(jnp.bfloat16)
    send(term_out.at[near], term_in.at[3], term_s.at[3, 0], term_r.at[3, 0], to_feat(partner))
    own_grad[...] = dot_nt(gpre[0], ws_ref[...])
    own_grad[...] += dot_tn(dense[SPAN], back[...])

    def send_terms():
        for c, at in enumerate(halves):
            value = term_sum[0, at, :]
            if square:
                landed(term_in.at[1, at], term_r.at[1, c])
                value = value + term_in[1, at, :].astype(jnp.float32)
            term_out[x_slot, at, :] = value.astype(jnp.bfloat16)
            if square:
                send(term_out.at[x_slot, at], term_in.at[0, at], term_s.at[2, c], term_r.at[0, c], to_feat(x_peer))
            else:
                target = lax.rem(me + x_slot - 2 + n_feat, n_feat)
                place = 1 - odd
                send(term_out.at[x_slot, at], term_in.at[place, at], term_s.at[2, c], term_r.at[place, c], to_feat(target))

    if not fine:
        send_terms()

    for q, (first, size) in enumerate(cuts):
        at = pl.ds(first, size)
        total = buf1[pl.ds(pl.multiple_of(chip * c2 + first, 16), size), :].astype(jnp.float32)
        for j in range(n_chip - 1):
            landed(in2.at[j, at], rs2_r.at[j, q])
            total = total + in2[j, at, :].astype(jnp.float32)
        buf2[at, :] = total.astype(jnp.bfloat16)
        if fine and q < n_grp - 1:
            send(buf2.at[at], in3.at[q], rs3_s.at[q], rs3_r.at[q], to_grp(grp_peers[q]))
    if fine:
        send_terms()
    else:
        for j, peer in enumerate(grp_peers):
            at = pl.ds(pl.multiple_of(peer * c3, c3), c3)
            send(buf2.at[at], in3.at[j], rs3_s.at[j], rs3_r.at[j], to_grp(peer))
    total = buf2[pl.ds(pl.multiple_of(grp * c3, c3), c3), :].astype(jnp.float32)
    for j in range(n_grp - 1):
        landed(in3.at[j], rs3_r.at[j])
        total = total + in3[j].astype(jnp.float32)

    def piece3(owner):
        return full.at[pl.ds(pl.multiple_of(core * half + chip * c2 + owner * c3, c3), c3)]

    def piece2(side, owner):
        return full.at[pl.ds(pl.multiple_of(side * half + owner * c2, c2), c2)]

    def spread_piece(owner, q):
        for j, peer in enumerate((x_peer, y_peer) if square else chip_peers):
            send(piece3(owner), piece3(owner), ag2_s.at[j, q], ag2_r.at[j, q], to_feat(peer))

    piece3(grp)[...] = total.astype(jnp.bfloat16)
    for j, peer in enumerate(grp_peers):
        send(piece3(grp), piece3(grp), ag3_s.at[j], ag3_r.at[j], to_grp(peer))
    if fine:
        spread_piece(grp, 0)
    for j in range(n_grp - 1):
        owner = lax.rem(grp + n_grp - 1 - j, n_grp)
        landed(piece3(owner), ag3_r.at[j])
        if fine:
            spread_piece(owner, j + 1)
    if not fine:
        for j, peer in enumerate(chip_peers):
            send(piece2(core, chip), piece2(core, chip), ag2_s.at[j, 0], ag2_r.at[j, 0], to_feat(peer))
    send(piece2(core, chip), piece2(core, chip), ag1_s.at[0], ag1_r.at[0], to_feat(partner))

    def piece_of(owner, q):
        if not fine:
            return piece2(core, owner)
        first = core * half + owner * c2 + lax.rem(grp + n_grp - q, n_grp) * c3
        return full.at[pl.ds(pl.multiple_of(first, c3), c3)]

    if square:
        sources = [x_peer // 2, y_peer // 2, lax.rem(x_peer // 2 + 2, n_chip)]
        for q in range(len(cuts)):
            for j in range(2):
                landed(piece_of(sources[j], q), ag2_r.at[j, q])
                if j == q % 2:
                    piece = piece_of(sources[j], q)
                    send(piece, piece, ag2_s.at[2, q], ag2_r.at[2, q], to_feat((y_peer, x_peer)[j]))
        for j in range(2):
            place = piece2(core, sources[j])
            send(place, place, ag1_s.at[j + 1], ag1_r.at[j + 1], to_feat(partner))
    else:
        sources = [lax.rem(chip + n_chip - 1 - j, n_chip) for j in range(n_chip - 1)]

    arrivals = (0, 3) if square else (0, 1, 3)
    for slot in arrivals:
        if slot == 3:
            landed(term_in.at[3], term_r.at[3, 0])
        else:
            for c, at in enumerate(halves):
                landed(term_in.at[slot, at], term_r.at[slot, c])

    def finish(at):
        grad = own_grad[at, :]
        for slot in arrivals:
            grad = grad + term_in[slot, at, :].astype(jnp.float32)
        gfeat_ref[at, :] = grad.astype(jnp.bfloat16)

    strips(rows, finish)
    store(gfeat_ref, gfeat_hbm)

    for j in range(2 if square else 0, n_chip - 1):
        for q in range(len(cuts)):
            landed(piece_of(sources[j], q), ag2_r.at[j, q])
        place = piece2(core, sources[j])
        send(place, place, ag1_s.at[j + 1], ag1_r.at[j + 1], to_feat(partner))
    own_half = pl.ds(pl.multiple_of(core * half, half), half)
    store(full.at[own_half], grads_hbm.at[own_half])
    for j, owner in enumerate([chip] + sources):
        landed(piece2(1 - core, owner), ag1_r.at[j])
    its_half = pl.ds(pl.multiple_of((1 - core) * half, half), half)
    store(full.at[its_half], grads_hbm.at[its_half])
    for copy in sent:
        copy.wait_send()
    for copy in stores:
        copy.wait()


def place_outputs(
    grad_scale, out_in, gfeat_in, grads_in, out_hbm, gfeat_hbm, self_hbm, neigh_hbm,
    held, scaled, out_held, gfeat_held, load_s, store_s
):
    part = held.shape[1]
    loads = [
        pltpu.make_async_copy(grads_in.at[pl.ds(i * part, part)], held.at[i], load_s.at[i]) for i in range(4)
    ]
    fetches = [
        pltpu.make_async_copy(out_in, out_held, load_s.at[4]),
        pltpu.make_async_copy(gfeat_in, gfeat_held, load_s.at[5]),
    ]
    for copy in loads + fetches:
        copy.start()
    moves = []
    for i in range(4):
        loads[i].wait()

        def widen(at, i=i):
            scaled[i, at, :] = held[i, at, :].astype(jnp.float32) * grad_scale

        strips(part, widen, 64)
        dst = (self_hbm, neigh_hbm)[i // 2].at[pl.ds((i % 2) * part, part)]
        store = pltpu.make_async_copy(scaled.at[i], dst, store_s.at[i])
        store.start()
        moves.append(store)
    for i, (src, dst) in enumerate(((out_held, out_hbm), (gfeat_held, gfeat_hbm))):
        fetches[i].wait()
        move = pltpu.make_async_copy(src, dst, store_s.at[4 + i])
        move.start()
        moves.append(move)
    for copy in moves:
        copy.wait()


def local(
    n_feat, n_grp, features, adj_tiles, src_block, counts, w_self, w_neigh, multiplier, bit_shift, cotangent
):
    rows, width = features.shape
    hidden = w_self.shape[1]
    n_chip = n_feat // 2
    lanes = hidden if width % (16 * n_chip * n_grp) == 0 else 128
    fine = n_chip * n_grp <= 16
    half = width * hidden // lanes
    c2 = half // n_chip
    c3 = c2 // n_grp
    bf, f32 = jnp.bfloat16, jnp.float32
    smem = pl.BlockSpec(memory_space=pltpu.SMEM)
    hbm = pl.BlockSpec(memory_space=pltpu.HBM)
    dma = pltpu.SemaphoreType.DMA
    cuts = n_grp if fine else 1
    output, grad_features, grads = pl.pallas_call(
        functools.partial(kernel, n_feat, n_grp, fine),
        out_shape=(
            jax.ShapeDtypeStruct((rows, hidden), bf),
            jax.ShapeDtypeStruct((rows, width), bf),
            jax.ShapeDtypeStruct((2 * half, lanes), bf),
        ),
        in_specs=[smem, smem] + [hbm] * 7,
        out_specs=(hbm, hbm, hbm),
        scratch_shapes=[
            pltpu.VMEM((rows, hidden), bf),
            pltpu.VMEM((rows, width), bf),
            pltpu.VMEM(adj_tiles.shape, bf),
            pltpu.VMEM(w_self.shape, bf),
            pltpu.VMEM(w_neigh.shape, bf),
            pltpu.VMEM((1, hidden), f32),
            pltpu.VMEM((1, hidden), jnp.int32),
            pltpu.VMEM((rows, hidden), bf),
            pltpu.VMEM((WIN, rows, width), bf),
            pltpu.VMEM((WIN, rows, rows), bf),
            pltpu.VMEM((rows, adj_tiles.shape[3]), f32),
            pltpu.VMEM((rows, 128), f32),
            pltpu.VMEM((rows, width), f32),
            pltpu.VMEM((rows, hidden), f32),
            pltpu.VMEM((4, rows, width), bf),
            pltpu.VMEM((2, rows, hidden), bf),
            pltpu.VMEM((half, lanes), bf),
            pltpu.VMEM((n_chip - 1, c2, lanes), bf),
            pltpu.VMEM((c2, lanes), bf),
            pltpu.VMEM((n_grp - 1, c3, lanes), bf),
            pltpu.VMEM((2 * half, lanes), bf),
            pltpu.VMEM((rows, width), bf),
            pltpu.VMEM((WIN, rows, width), bf),
            pltpu.VMEM((2, rows, width), f32),
            pltpu.VMEM((rows, width), f32),
            pltpu.VMEM((4, rows, width), bf),
            dma((7,)), dma((4,)), dma((4, CHUNKS)), dma((WIN, CHUNKS)), dma((4, 2)), dma((4, 2)),
            dma((3,)), dma((3,)), dma((n_chip - 1, cuts)), dma((n_chip - 1, cuts)),
            dma((n_grp - 1,)), dma((n_grp - 1,)),
            dma((n_chip,)), dma((n_chip,)), dma((n_chip - 1, cuts)), dma((n_chip - 1, cuts)),
            dma((n_grp - 1,)), dma((n_grp - 1,)),
        ],
        compiler_params=pltpu.CompilerParams(
            collective_id=0, has_side_effects=True, vmem_limit_bytes=62 * 1024 * 1024
        ),
    )(
        src_block, counts, features, adj_tiles, w_self, w_neigh,
        multiplier.reshape(1, hidden), bit_shift.reshape(1, hidden), cotangent,
    )
    grad_scale = 1.0 / math.sqrt(rows * n_grp * n_feat)
    if lanes != hidden:
        grads = grads.reshape(2, hidden // lanes, width, lanes).transpose(0, 2, 1, 3).reshape(2 * width, hidden)
    return pl.pallas_call(
        functools.partial(place_outputs, grad_scale),
        out_shape=(
            jax.ShapeDtypeStruct(output.shape, bf),
            jax.ShapeDtypeStruct(grad_features.shape, bf),
            jax.ShapeDtypeStruct((width, hidden), f32),
            jax.ShapeDtypeStruct((width, hidden), f32),
        ),
        in_specs=[hbm] * 3,
        out_specs=(hbm,) * 4,
        scratch_shapes=[
            pltpu.VMEM((4, width // 2, hidden), bf),
            pltpu.VMEM((4, width // 2, hidden), f32),
            pltpu.VMEM(output.shape, bf),
            pltpu.VMEM(grad_features.shape, bf),
            dma((6,)),
            dma((6,)),
        ],
        compiler_params=pltpu.CompilerParams(vmem_limit_bytes=62 * 1024 * 1024),
    )(output, grad_features, grads)


def solution(mesh):
    return jax.shard_map(
        functools.partial(local, mesh.shape["feat"], mesh.shape["grp"]),
        mesh=mesh,
        in_specs=(
            P(("grp", "feat"), None),
            P(("grp", "feat"), None, None, None),
            P(("grp", "feat"), None),
            P(("grp", "feat")),
            P(),
            P(),
            P(),
            P(),
            P(("grp", "feat"), None),
        ),
        out_specs=(P(("grp", "feat"), None), P(("grp", "feat"), None), P(), P()),
        check_vma=False,
    )
```

profile of v0, /device:TPU:1, one launch (start us, length us, event | category | flops | bytes accessed | tf_op | source)
XLA Modules:
  0.0 49.9 jit_solution(11056700058746997191)
XLA Ops:
  0.6 46.6 %shard_map.120 = (bf16[256,512]{1,0:T(8,128)(2,1)}, bf16[256,512]{1,0:T(8,128)(2,1)}, bf16[1024,512]{1,0:T(8,128)(2,1)}) custom-call(s32[2,16]{1,0:T(2,128)} %src_ref.1, s32[2]{0:T(128)} %cnt_ref.1, bf16[256,512]{1,0:T(8,128)(2,1)} %feat_hbm.1, bf16[2,16,128,128]{3,2,1,0:T(8,128)(2,1)} %adj_hbm.1, bf16[512,512]{1,0:T(8,128)(2,1)} %ws_hbm.1, ...), custom_call_target="tpu_custom_call" | custom-call | tf_op jit(solution)/shard_map/pallas_call | solution.py:421
  47.3 2.6 %shard_map.121 = (bf16[256,512]{1,0:T(8,128)(2,1)}, bf16[256,512]{1,0:T(8,128)(2,1)}, f32[512,512]{1,0:T(8,128)}, f32[512,512]{1,0:T(8,128)}) custom-call(bf16[256,512]{1,0:T(8,128)(2,1)} %get-tuple-element.7.out_in, bf16[256,512]{1,0:T(8,128)(2,1)} %get-tuple-element.8.gfeat_in, bf16[1024,512]{1,0:T(8,128)(2,1)} %get-tuple-element.9.grads_in), custom_call_target="tpu_custom_call" | custom-call | tf_op jit(solution)/shard_map/pallas_call | solution.py:473
where the time goes:
time: 50.1 us; the launch traced here: 49.9 us
  Pallas kernels  49.2 us (98%)
  between operations  0.64 us (1%)
    pallas_call x1, Pallas kernels, local(): pl.pallas_call(functools.partial(kernel, n_feat, n_grp, fine), out_shape=...  46.6 us
    pallas_call x1, Pallas kernels, local(): pl.pallas_call(functools.partial(place_outputs, grad_scale), out_shape=(j...  2.59 us

commit v1 on v0

--- a/solution.py
+++ b/solution.py
@@ -13,7 +13,6 @@
 MESH = pl.DeviceIdType.MESH
 STRIP = 32
 CHUNKS = 8
-SPLIT = 3
 
 
 def dot_nn(a, b):
@@ -38,9 +37,9 @@
 
 def kernel(
     n_feat, n_grp, fine,
-    src_ref, cnt_ref, feat_hbm, adj_hbm, ws_hbm, wn_hbm, mult_hbm, shift_hbm, cot_hbm,
+    src_hbm, cnt_hbm, feat_hbm, adj_hbm, ws_hbm, wn_hbm, mult_hbm, shift_hbm, cot_hbm,
     out_hbm, gfeat_hbm, grads_hbm,
-    out_ref, gfeat_ref,
+    src_ref, cnt_ref, out_ref, gfeat_ref,
     adj_ref, ws_ref, wn_ref, mult_ref, shift_ref, cot_ref,
     pool, dense, dsum, inv, summed, preact, both, gpre,
     buf1, in2, buf2, in3, full,
@@ -95,6 +94,7 @@
             (
                 (feat_hbm, both.at[0]), (adj_hbm, adj_ref), (ws_hbm, ws_ref), (wn_hbm, wn_ref),
                 (mult_hbm, mult_ref), (shift_hbm, shift_ref), (cot_hbm, cot_ref),
+                (src_hbm, src_ref), (cnt_hbm, cnt_ref),
             )
         )
     ]
@@ -123,9 +123,10 @@
     send(both.at[0], both.at[2], halo_s.at[2, 0], halo_r.at[SPAN, 0], to_feat(partner))
 
     dsum[...] = jnp.zeros_like(dsum)
-    loads[1].wait()
-
-    def build(piece, carry):
+    for load in (loads[1], loads[7], loads[8]):
+        load.wait()
+
+    def build(piece):
         owner = lax.rem(me + piece - SPAN + n_feat, n_feat)
         for b in range(num_blocks):
             dst_rows = slice(b * block_len, (b + 1) * block_len)
@@ -137,29 +138,34 @@
                     acc = acc + adj_ref[b, k].astype(jnp.float32) * jnp.where(hit, 1.0, 0.0)
                 dsum[dst_rows, :] += acc
                 dense[piece, dst_rows, h * block_len : (h + 1) * block_len] = acc.astype(jnp.bfloat16)
-        return carry
-
-    def relay():
-        for c, at in enumerate(chunks):
-            landed(pool.at[x_slot, at], halo_r.at[x_slot, c])
-            if square:
-                send(pool.at[x_slot, at], pool.at[y_slot, at], halo_s.at[1, c], halo_r.at[y_slot, c], to_feat(y_peer))
-
-    lax.fori_loop(0, SPLIT, build, 0)
-    relay()
-    lax.fori_loop(SPLIT, WIN, build, 0)
-    inv[...] = jnp.broadcast_to(lax.rsqrt(jnp.sum(dsum[...], axis=1, keepdims=True)), inv.shape)
-    loads[2].wait()
-    preact[...] = dot_nn(both[0], ws_ref[...])
-    summed[...] = dot_nn(dense[SPAN], both[0])
-    landed(both.at[2], halo_r.at[SPAN, 0])
-    summed[...] += dot_nn(dense[near], both[2])
+
+    def norms():
+        inv[...] = jnp.broadcast_to(lax.rsqrt(jnp.sum(dsum[...], axis=1, keepdims=True)), inv.shape)
+
+    def own_preact():
+        loads[2].wait()
+        preact[...] = dot_nn(both[0], ws_ref[...])
+
+    def own_rows():
+        summed[...] = dot_nn(dense[SPAN], both[0])
+
+    def near_rows():
+        landed(both.at[2], halo_r.at[SPAN, 0])
+        summed[...] += dot_nn(dense[near], both[2])
+
+    work = [functools.partial(build, piece) for piece in range(WIN)] + [norms, own_preact, own_rows, near_rows]
+    work.pop(0)()
+    for c, at in enumerate(chunks):
+        work.pop(0)()
+        landed(pool.at[x_slot, at], halo_r.at[x_slot, c])
+        if square:
+            send(pool.at[x_slot, at], pool.at[y_slot, at], halo_s.at[1, c], halo_r.at[y_slot, c], to_feat(y_peer))
     summed[...] += dot_nn(dense[x_slot], pool[x_slot])
     for c, at in enumerate(chunks):
         landed(pool.at[y_slot, at], halo_r.at[y_slot, c])
         send(pool.at[far, at], pool.at[near, at], halo_s.at[3, c], halo_r.at[near, c], to_feat(partner))
     summed[...] += dot_nn(dense[y_slot], pool[y_slot])
-    for load in loads[3:]:
+    for load in loads[3:7]:
         load.wait()
     for c, at in enumerate(chunks):
         landed(pool.at[passed, at], halo_r.at[passed, c])
@@ -175,6 +181,7 @@
 
     tstep = rows // 2
     halves = [pl.ds(c * tstep, tstep) for c in range(2)]
+    quarters = [pl.ds(c * (rows // 4), rows // 4) for c in range(4)]
 
     def activate(at):
         scale = mult_ref[...]
@@ -239,7 +246,7 @@
     landed(term_in.at[2], term_r.at[2, 0])
     through = lax.rem(core + chip, 2)
     term_sum[through] += term_in[2].astype(jnp.float32)
-    for c, at in enumerate(halves):
+    for c, at in enumerate(quarters):
         term_out[y_slot, at, :] = term_sum[1, at, :].astype(jnp.bfloat16)
         if square:
             send(term_out.at[y_slot, at], term_in.at[1, at], term_s.at[1, c], term_r.at[1, c], to_feat(y_peer))
@@ -252,7 +259,7 @@
     own_grad[...] += dot_tn(dense[SPAN], back[...])
 
     def send_terms():
-        for c, at in enumerate(halves):
+        for c, at in enumerate(quarters):
             value = term_sum[0, at, :]
             if square:
                 landed(term_in.at[1, at], term_r.at[1, c])
@@ -338,7 +345,7 @@
         if slot == 3:
             landed(term_in.at[3], term_r.at[3, 0])
         else:
-            for c, at in enumerate(halves):
+            for c, at in enumerate(quarters):
                 landed(term_in.at[slot, at], term_r.at[slot, c])
 
     def finish(at):
@@ -414,7 +421,6 @@
     c2 = half // n_chip
     c3 = c2 // n_grp
     bf, f32 = jnp.bfloat16, jnp.float32
-    smem = pl.BlockSpec(memory_space=pltpu.SMEM)
     hbm = pl.BlockSpec(memory_space=pltpu.HBM)
     dma = pltpu.SemaphoreType.DMA
     cuts = n_grp if fine else 1
@@ -425,9 +431,11 @@
             jax.ShapeDtypeStruct((rows, width), bf),
             jax.ShapeDtypeStruct((2 * half, lanes), bf),
         ),
-        in_specs=[smem, smem] + [hbm] * 7,
+        in_specs=[hbm] * 9,
         out_specs=(hbm, hbm, hbm),
         scratch_shapes=[
+            pltpu.SMEM(src_block.shape, jnp.int32),
+            pltpu.SMEM(counts.shape, jnp.int32),
             pltpu.VMEM((rows, hidden), bf),
             pltpu.VMEM((rows, width), bf),
             pltpu.VMEM(adj_tiles.shape, bf),
@@ -454,7 +462,7 @@
             pltpu.VMEM((2, rows, width), f32),
             pltpu.VMEM((rows, width), f32),
             pltpu.VMEM((4, rows, width), bf),
-            dma((7,)), dma((4,)), dma((4, CHUNKS)), dma((WIN, CHUNKS)), dma((4, 2)), dma((4, 2)),
+            dma((9,)), dma((4,)), dma((4, CHUNKS)), dma((WIN, CHUNKS)), dma((4, 4)), dma((4, 4)),
             dma((3,)), dma((3,)), dma((n_chip - 1, cuts)), dma((n_chip - 1, cuts)),
             dma((n_grp - 1,)), dma((n_grp - 1,)),
             dma((n_chip,)), dma((n_chip,)), dma((n_chip - 1, cuts)), dma((n_chip - 1, cuts)),

time: 50.1 us -> 49.5 us (0.988)
    pallas_call x1, Pallas kernels: 46.6 us -> 46.1 us  [local(): pl.pallas_call(functools.partial(kernel, n_feat, n_grp, fine), out_shape=...]
where the time goes in v1:
time: 49.5 us; the launch traced here: 49.4 us
  Pallas kernels  48.7 us (98%)
  between operations  0.64 us (1%)
    pallas_call x1, Pallas kernels, local(): pl.pallas_call(functools.partial(kernel, n_feat, n_grp, fine), out_shape=...  46.1 us
    pallas_call x1, Pallas kernels, local(): pl.pallas_call(functools.partial(place_outputs, grad_scale), out_shape=(j...  2.59 us

profile of v1, /device:TPU:1, one launch (start us, length us, event | category | flops | bytes accessed | tf_op | source)
XLA Modules:
  0.0 49.4 jit_solution(9626160513882017766)
XLA Ops:
  0.6 46.1 %shard_map.120 = (bf16[256,512]{1,0:T(8,128)(2,1)}, bf16[256,512]{1,0:T(8,128)(2,1)}, bf16[1024,512]{1,0:T(8,128)(2,1)}) custom-call(s32[2,16]{1,0:T(2,128)} %src_hbm.1, s32[2]{0:T(128)} %cnt_hbm.1, bf16[256,512]{1,0:T(8,128)(2,1)} %feat_hbm.1, bf16[2,16,128,128]{3,2,1,0:T(8,128)(2,1)} %adj_hbm.1, bf16[512,512]{1,0:T(8,128)(2,1)} %ws_hbm.1, ...), custom_call_target="tpu_custom_call" | custom-call | tf_op jit(solution)/shard_map/pallas_call | solution.py:427
  46.8 2.6 %shard_map.121 = (bf16[256,512]{1,0:T(8,128)(2,1)}, bf16[256,512]{1,0:T(8,128)(2,1)}, f32[512,512]{1,0:T(8,128)}, f32[512,512]{1,0:T(8,128)}) custom-call(bf16[256,512]{1,0:T(8,128)(2,1)} %get-tuple-element.7.out_in, bf16[256,512]{1,0:T(8,128)(2,1)} %get-tuple-element.8.gfeat_in, bf16[1024,512]{1,0:T(8,128)(2,1)} %get-tuple-element.9.grads_in), custom_call_target="tpu_custom_call" | custom-call | tf_op jit(solution)/shard_map/pallas_call | solution.py:481

commit v2 on v1

--- a/solution.py
+++ b/solution.py
@@ -272,8 +272,7 @@
                 place = 1 - odd
                 send(term_out.at[x_slot, at], term_in.at[place, at], term_s.at[2, c], term_r.at[place, c], to_feat(target))
 
-    if not fine:
-        send_terms()
+    send_terms()
 
     for q, (first, size) in enumerate(cuts):
         at = pl.ds(first, size)
@@ -284,9 +283,7 @@
         buf2[at, :] = total.astype(jnp.bfloat16)
         if fine and q < n_grp - 1:
             send(buf2.at[at], in3.at[q], rs3_s.at[q], rs3_r.at[q], to_grp(grp_peers[q]))
-    if fine:
-        send_terms()
-    else:
+    if not fine:
         for j, peer in enumerate(grp_peers):
             at = pl.ds(pl.multiple_of(peer * c3, c3), c3)
             send(buf2.at[at], in3.at[j], rs3_s.at[j], rs3_r.at[j], to_grp(peer))

time: 49.5 us -> 54.8 us (1.11)
  Pallas kernels: 48.7 us -> 54 us
    pallas_call x1, Pallas kernels: 46.1 us -> 51.4 us  [local(): pl.pallas_call(functools.partial(kernel, n_feat, n_grp, fine), out_shape=...]
where the time goes in v2:
time: 54.8 us; the launch traced here: 54.6 us
  Pallas kernels  54 us (99%)
  between operations  0.64 us (1%)
    pallas_call x1, Pallas kernels, local(): pl.pallas_call(functools.partial(kernel, n_feat, n_grp, fine), out_shape=...  51.4 us
    pallas_call x1, Pallas kernels, local(): pl.pallas_call(functools.partial(place_outputs, grad_scale), out_shape=(j...  2.59 us

profile of v2, /device:TPU:1, one launch (start us, length us, event | category | flops | bytes accessed | tf_op | source)
XLA Modules:
  0.0 54.6 jit_solution(6068276990927501678)
XLA Ops:
  0.6 51.4 %shard_map.120 = (bf16[256,512]{1,0:T(8,128)(2,1)}, bf16[256,512]{1,0:T(8,128)(2,1)}, bf16[1024,512]{1,0:T(8,128)(2,1)}) custom-call(s32[2,16]{1,0:T(2,128)} %src_hbm.1, s32[2]{0:T(128)} %cnt_hbm.1, bf16[256,512]{1,0:T(8,128)(2,1)} %feat_hbm.1, bf16[2,16,128,128]{3,2,1,0:T(8,128)(2,1)} %adj_hbm.1, bf16[512,512]{1,0:T(8,128)(2,1)} %ws_hbm.1, ...), custom_call_target="tpu_custom_call" | custom-call | tf_op jit(solution)/shard_map/pallas_call | solution.py:424
  52.1 2.6 %shard_map.121 = (bf16[256,512]{1,0:T(8,128)(2,1)}, bf16[256,512]{1,0:T(8,128)(2,1)}, f32[512,512]{1,0:T(8,128)}, f32[512,512]{1,0:T(8,128)}) custom-call(bf16[256,512]{1,0:T(8,128)(2,1)} %get-tuple-element.7.out_in, bf16[256,512]{1,0:T(8,128)(2,1)} %get-tuple-element.8.gfeat_in, bf16[1024,512]{1,0:T(8,128)(2,1)} %get-tuple-element.9.grads_in), custom_call_target="tpu_custom_call" | custom-call | tf_op jit(solution)/shard_map/pallas_call | solution.py:478
